TPU v7x, 256 devices: a whole 4x4x8 slice. The times are simulated.
256 devices in a mesh: member: 8 (over y, core), dp: 16 (over z_lo, x), owner: 2 (over z_hi).
Axes of the slice: x: 4, y: 4, z: 8 (z_hi: 2, z_lo: 4; z = z_hi * 4 + z_lo), core: 2. Of those that a mesh axis runs over, the one named last changes fastest.
Arguments:
- factor_rows: bfloat16 [2, 32768, 8192], P('owner', ('member', 'dp')), parts along dimension 1, may hold values from -50 to 50, as said below
- feature_order: int32 [2, 8192], P('owner'), may hold values from 0 to 8191, each once within a row
- gradients: bfloat16 [2, 8192, 16384], P('owner', None, ('member', 'dp')), parts along dimension 2, may hold values from -6 to 6
Outputs:
- preconditioned: bfloat16 [2, 8192, 16384], P('owner', None, ('member', 'dp')), parts along dimension 2
There are 8 independent parts, one for each index of `member`. A program takes and returns all parts, laid end to end along the dimension named above; an argument that names none is the same for every part. Nothing has to cross between parts.
Inputs may be any that keep to these rules, and one draw needn't show every extreme that they name: `factor_rows`: real-valued data, column scales differing across hidden units. `feature_order`: each row is a permutation of 0 to 8191.
All inputs are finite; a program needn't handle non-finite values. Where the computation divides by a largest or mean magnitude, that divisor is 1e-20 or more.
Results may differ from a plain program's by a relative error of at most 0.005.
Values may be sent and summed in bfloat16 or wider, within the bound.
No kernel may reach another device: no remote copies, remote signals or barrier semaphores. Data moves between devices by JAX's collectives and lax.ppermute only.
A program may use at most 128 MiB of HBM per device.

v0:
```python
import jax
import jax.numpy as jnp
from jax import lax
from jax.sharding import PartitionSpec as P

BLK = 512
NS_STEPS = 12


DAMPING = 0.001


def shards(factor_rows, feature_order, gradients):
    data_rows = factor_rows[0]
    feature_perm = feature_order[0]
    grad_rows = gradients[0]
    group_size = lax.axis_size("dp")
    tok_rows = data_rows.shape[0]
    feature_count = data_rows.shape[1]
    block_count = feature_count // BLK
    owned_count = block_count // group_size
    permuted = jnp.take(data_rows, feature_perm, axis=1).reshape(tok_rows, block_count, BLK)
    product = jnp.einsum("tki,tkj->kij", permuted, permuted, preferred_element_type=jnp.float32)
    summed = lax.psum_scatter(
        product.reshape(owned_count * BLK * lax.axis_size("dp"), BLK),
        "dp",
        scatter_dimension=0,
        tiled=True,
    )
    covariance = summed.reshape(owned_count, BLK, BLK)
    covariance = covariance / float(tok_rows * group_size)
    identity = jnp.eye(BLK, dtype=jnp.float32)
    damped = covariance + DAMPING * identity
    step_scale = 1.0 / jnp.max(jnp.sum(jnp.abs(damped), axis=2), axis=1)
    approx = step_scale[:, None, None] * identity

    def newton_step(iteration, current):
        product = jnp.einsum("kij,kjl->kil", damped, current, precision=lax.Precision.HIGHEST)
        return jnp.einsum(
            "kij,kjl->kil", current, 2.0 * identity - product, precision=lax.Precision.HIGHEST
        )

    approx = lax.fori_loop(0, NS_STEPS, newton_step, approx)
    inverse = approx.astype(jnp.bfloat16)
    grad_perm = jnp.take(grad_rows, feature_perm, axis=0).reshape(
        block_count, BLK, grad_rows.shape[1]
    )
    result = jnp.einsum(
        "kij,kjd->kid",
        lax.all_gather(inverse, "dp", axis=0, tiled=True),
        grad_perm,
        preferred_element_type=jnp.float32,
    ).astype(jnp.bfloat16)
    flat_result = result.reshape(feature_count, grad_rows.shape[1])
    restored = (
        jnp.zeros((feature_count, grad_rows.shape[1]), jnp.bfloat16)
        .at[feature_perm]
        .set(flat_result)
    )
    return restored[None]


def solution(mesh):
    return jax.shard_map(
        shards,
        mesh=mesh,
        in_specs=(
            P("owner", ("member", "dp"), None),
            P("owner", None),
            P("owner", None, ("member", "dp")),
        ),
        out_specs=P("owner", None, ("member", "dp")),
        check_vma=False,
    )
```

profile of v0, /device:TPU:1, one launch (start us, length us, event | category | flops | bytes accessed | tf_op | source)
XLA Modules:
  0.0 451.1 jit_solution(7887395937399357954)
XLA Ops:
  7.5 6.4 %copy.10 = bf16[1,256,8192]{1,2,0:T(8,128)(2,1)} copy(bf16[1,256,8192]{2,1,0:T(8,128)(2,1)} %param.5) | data formatting | bytes 8388608 | tf_op args[0]
  15.2 33.6 %gather_fusion = bf16[8192,256]{1,0:T(8,128)(2,1)} fusion(bf16[256,8192]{0,1:T(8,128)(2,1)} %bitcast.39, s32[8192]{0:T(1024)S(1)} %broadcast_clamp_fusion), kind=kCustom, calls=%fused_computation | custom fusion | bytes 8421376 | tf_op jit(solution)/shard_map/jit(_take)/gather | solution.py:22
  48.8 11.2 %fusion.5 = f32[16,512,512]{2,1,0:T(8,128)} fusion(bf16[256,16,512]{0,2,1:T(8,128)(2,1)} %bitcast.41, pred[16,512]{1,0:T(8,128)(4,1)S(1)} %compare_and_fusion), kind=kOutput, calls=%fused_computation.10 | convolution fusion | flops 2149580800 | bytes 20979712 | tf_op jit(solution)/shard_map/tki,tkj->kij/dot_general | solution.py:23
  60.1 191.1 %reduce-scatter.2.cloned.1.call-done = f32[512,512]{1,0:T(8,128)} async-done(((f32[8192,512]{1,0:T(8,128)}), f32[512,512]{1,0:T(8,128)}) %reduce-scatter.2.cloned.1.call-update) | async-done | bytes 1048592 | tf_op jit(solution)/shard_map/reduce_scatter | solution.py:24
  251.2 2.3 fusion.19
  255.0 59.6 %while.11 = (s32[]{:T(128)}, f32[1,512,512]{1,2,0:T(8,128)S(1)}, f32[1,512,512]{2,1,0:T(8,128)}, s32[]{:T(128)}) while((s32[]{:T(128)}, f32[1,512,512]{1,2,0:T(8,128)S(1)}, f32[1,512,512]{2,1,0:T(8,128)}, s32[]{:T(128)}) %tuple.22), condition=%wide.region_4.5_spmd.clone, body=%wide.region_3.4_spmd.clone.sunk | while | flops 3222011904 | bytes 12582993 | solution.py:43
  256.3 1.9 convolution_subtract_fusion.2
  258.1 1.8 convolution_bitcast_fusion.2
  261.2 1.9 convolution_subtract_fusion.2
  263.1 1.8 convolution_bitcast_fusion.2
  266.2 1.9 convolution_subtract_fusion.2
  271.2 1.9 convolution_subtract_fusion.2
  273.0 1.9 convolution_bitcast_fusion.2
  276.1 1.9 convolution_subtract_fusion.2
  281.1 1.9 convolution_subtract_fusion.2
  283.0 1.9 convolution_bitcast_fusion.2
  286.1 1.9 convolution_subtract_fusion.2
  287.9 1.8 convolution_bitcast_fusion.2
  291.0 1.9 convolution_subtract_fusion.2
  292.9 1.9 convolution_bitcast_fusion.2
  296.0 1.9 convolution_subtract_fusion.2
  297.9 1.8 convolution_bitcast_fusion.2
  301.0 1.9 convolution_subtract_fusion.2
  302.8 1.9 convolution_bitcast_fusion.2
  305.9 1.9 convolution_subtract_fusion.2
  307.8 1.8 convolution_bitcast_fusion.2
  310.9 1.9 convolution_subtract_fusion.2
  312.8 1.9 convolution_bitcast_fusion.2
  315.7 29.5 %gather_fusion.1 = bf16[8192,128]{1,0:T(8,128)(2,1)} fusion(bf16[8192,128]{1,0:T(8,128)(2,1)S(1)} %bitcast.38, s32[8192]{0:T(1024)S(1)} %broadcast_clamp_fusion), kind=kCustom, calls=%fused_computation.1 | custom fusion | bytes 4227072 | tf_op jit(solution)/shard_map/jit(_take)/gather | solution.py:45
  345.2 69.9 %all-gather.2.cloned.1.call-done = bf16[16,512,512]{2,1,0:T(8,128)(2,1)} async-done(((bf16[1,512,512]{2,1,0:T(8,128)(2,1)}), bf16[16,512,512]{2,1,0:T(8,128)(2,1)}) %all-gather.2.cloned.1.call-update) | async-done | bytes 8388624 | tf_op jit(solution)/shard_map/all_gather | solution.py:50
  415.1 6.3 %fusion.12 = bf16[16,512,128]{2,1,0:T(8,128)(2,1)} fusion(bf16[16,512,512]{2,1,0:T(8,128)(2,1)} %all-gather.2.cloned.1.call-done, bf16[16,512,128]{2,1,0:T(8,128)(2,1)} %bitcast.42, pred[16,512]{1,0:T(8,128)(4,1)S(1)} %compare_and_fusion), kind=kOutput, calls=%fused_computation.17 | convolution fusion | flops 1075838976 | bytes 12591104 | tf_op jit(solution)/shard_map/kij,kjd->kid/dot_general | solution.py:48
  421.4 22.8 %scatter_custom_fusion = bf16[8192,128]{1,0:T(8,128)(2,1)} fusion(s32[8192]{0:T(1024)S(1)} %bitcast.44, bf16[8192,128]{1,0:T(8,128)(2,1)} %bitcast.45, bf16[]{:T(256)} %constant.28.clone.1), kind=kCustom, calls=%fused_computation.23 | custom fusion | bytes 2097664 | tf_op jit(solution)/shard_map/scatter | solution.py:58
  (55 shorter events, 22.4 us)
Async XLA Ops:
  6.5 309.2 %copy-start = (bf16[1,8192,128]{2,1,0:T(8,128)(2,1)S(1)}, bf16[1,8192,128]{2,1,0:T(8,128)(2,1)}, u32[]{:S(2)}) copy-start(bf16[1,8192,128]{2,1,0:T(8,128)(2,1)} %param.7) | copy-start | bytes 6291460
  6.5 244.6 %reduce-scatter.2.cloned.1.call-start = ((), (), s32[]{:S(2)}) async-start(), calls=%async_computation.1 | async-start | bytes 17825792 | tf_op jit(solution)/shard_map/reduce_scatter | solution.py:24
  7.5 6.9 %copy-start.2 = (s32[1,8192]{1,0:T(1,128)S(1)}, s32[1,8192]{1,0:T(1,128)}, u32[]{:S(2)}) copy-start(s32[1,8192]{1,0:T(1,128)} %param.6) | copy-start | bytes 98308
  60.0 355.1 %all-gather.2.cloned.1.call-start = ((), (), s32[]{:S(2)}) async-start(), calls=%async_computation.2 | async-start | bytes 8912896 | tf_op jit(solution)/shard_map/all_gather | solution.py:50
  255.0 1.2 copy-start.1
  260.0 1.2 copy-start.1
  265.0 1.2 copy-start.1
  269.9 1.2 copy-start.1
  274.9 1.2 copy-start.1
  279.9 1.2 copy-start.1
  284.8 1.2 copy-start.1
  289.8 1.2 copy-start.1
  294.8 1.2 copy-start.1
  299.7 1.2 copy-start.1
  304.7 1.2 copy-start.1
  309.7 1.2 copy-start.1
Sparse Core Ops, SparseCore 0:
  60.1 190.9 reduce-scatter.1
  315.8 99.1 all-gather.1
where the time goes:
time: 452 us; the launch traced here: 451 us
  waiting for transfers between devices  261 us (58%)
  local copies, waits for them, and re-layouts  108 us (24%)
  matrix products  62 us (14%)
  between operations  14.2 us (3%)
  other arithmetic  4.81 us (1%)
    reduce_scatter x1, waiting for transfers between devices, shards(): lax.psum_scatter(product.reshape(owned_count * BLK * lax.axis_size('dp'),...  191 us
    all_gather x1, waiting for transfers between devices, shards(): lax.all_gather(inverse, 'dp', axis=0, tiled=True)  69.9 us
    gather x1, local copies, waits for them, and re-layouts, shards(): jnp.take(data_rows, feature_perm, axis=1)  33.6 us
    gather x1, local copies, waits for them, and re-layouts, shards(): jnp.take(grad_rows, feature_perm, axis=0)  29.5 us
    scatter x1, local copies, waits for them, and re-layouts, shards(): restored = jnp.zeros((feature_count, grad_rows.shape[1]), jnp.bfloat16).a...  22.8 us
    dot_general x12, matrix products, newton_step(): jnp.einsum('kij,kjl->kil', damped, current, precision=lax.Precision.HIGHEST)  22.3 us
    dot_general x12, matrix products, newton_step(): jnp.einsum('kij,kjl->kil', current, 2.0 * identity - product, precision=l...  22.2 us
    while x36, local copies, waits for them, and re-layouts  14.5 us
  transfers between devices with their start and end apart: 2, of which 2 were waited for; matrix products, arithmetic and copies ran while one was open for 7% of the time, Pallas kernels for 0%

commit v1 on v0

v1 whole, which is shorter than its diff:
```python
import functools

import jax
import jax.numpy as jnp
from jax import lax
from jax.experimental import pallas as pl
from jax.experimental.pallas import tpu as pltpu
from jax.sharding import PartitionSpec as P

BLK = 512
NS_STEPS = 12
DAMPING = 0.001
TILE = 128
LANES = 128
SIDE = BLK // TILE
UPPER = [(r, c) for r in range(SIDE) for c in range(r + 1, SIDE)]
DIAGONAL = [(r, r + 1) for r in range(0, SIDE, 2)]
TAIL = (len(UPPER) + len(DIAGONAL)) * TILE
PACKED = TAIL + 16
RING = 4
LINE = 4
UNROLL = 64
PHASES = (3, 2, 1, 0)

VMEM = pl.BlockSpec(memory_space=pltpu.VMEM)
SMEM = pl.BlockSpec(memory_space=pltpu.SMEM)
ANY = pl.BlockSpec(memory_space=pl.ANY)
PARAMS = pltpu.CompilerParams(vmem_limit_bytes=48 * 1024 * 1024)


def ring_shift(value, step):
    pairs = [
        (z * RING + x, z * RING + (x + step) % RING) for z in range(LINE) for x in range(RING)
    ]
    return lax.ppermute(value, "dp", pairs)


def line_swap(value, mask):
    pairs = [(z * RING + x, (z ^ mask) * RING + x) for z in range(LINE) for x in range(RING)]
    return lax.ppermute(value, "dp", pairs)


def block_start(phase, offset):
    place = lax.axis_index("dp")
    z = lax.div(place, RING)
    x = lax.rem(place, RING)
    block = lax.bitwise_xor(z, phase) * RING + lax.rem(x + offset, RING)
    return block * BLK


def gather_rows(order, start, sources, targets):
    def step(group, carry):
        first = pl.multiple_of(group * UNROLL, UNROLL)
        for inner in range(UNROLL):
            row = order[0, start + first + inner]
            for source, target in zip(sources, targets):
                target[pl.ds(first + inner, 1), :] = source[pl.ds(row, 1), :]
        return carry

    lax.fori_loop(0, BLK // UNROLL, step, 0)


def pick_columns_kernel(phases, order, rows, *refs):
    outs, turned, picked = refs[-RING - 4 : -4], refs[-4:-2], refs[-2:]
    width = 256
    for first in range(0, rows.shape[1], width):
        part = rows[:, first : first + width].astype(jnp.float32).T
        for half, target in enumerate(turned):
            target[first : first + width, :] = part[:, half * LANES : (half + 1) * LANES]
    for offset in range(RING):
        for place, phase in enumerate(phases):
            gather_rows(order, block_start(phase, offset), turned, picked)
            for half, source in enumerate(picked):
                outs[offset][
                    place * BLK : (place + 1) * BLK, half * LANES : (half + 1) * LANES
                ] = source[...].astype(jnp.bfloat16)


def pick_columns(phases, order, rows, after=()):
    tokens, features = rows.shape
    return pl.pallas_call(
        functools.partial(pick_columns_kernel, phases),
        out_shape=[jax.ShapeDtypeStruct((len(phases) * BLK, tokens), jnp.bfloat16)] * RING,
        in_specs=[SMEM, VMEM] + [ANY] * len(after),
        out_specs=[VMEM] * RING,
        scratch_shapes=[pltpu.VMEM((features, LANES), jnp.float32)] * 2
        + [pltpu.VMEM((BLK, LANES), jnp.float32)] * 2,
        compiler_params=PARAMS,
        name="pick_columns",
    )(order, rows, *after)


def pick_grads_kernel(order, grads, *refs):
    outs, (wide, picked) = refs[-2 - RING : -2], refs[-2:]
    wide[...] = grads[...].astype(jnp.float32)
    for place, phase in enumerate(PHASES):
        for offset in range(RING):
            gather_rows(order, block_start(phase, offset), [wide], [picked])
            outs[offset][place * BLK : (place + 1) * BLK, :] = picked[...].astype(jnp.bfloat16)


def pick_grads(order, grads, after=()):
    features, columns = grads.shape
    return pl.pallas_call(
        pick_grads_kernel,
        out_shape=[jax.ShapeDtypeStruct((LINE * BLK, columns), jnp.bfloat16)] * RING,
        in_specs=[SMEM, VMEM] + [ANY] * len(after),
        out_specs=[VMEM] * RING,
        scratch_shapes=[
            pltpu.VMEM((features, columns), jnp.float32),
            pltpu.VMEM((BLK, columns), jnp.float32),
        ],
        compiler_params=PARAMS,
        name="pick_grads",
    )(order, grads, *after)


def tile_indices():
    rows = lax.broadcasted_iota(jnp.int32, (TILE, TILE), 0)
    columns = lax.broadcasted_iota(jnp.int32, (TILE, TILE), 1)
    return rows, columns


def pack(tile_at):
    rows, columns = tile_indices()
    parts = [tile_at(r, c) for r, c in UPPER]
    tails = []
    for first, second in DIAGONAL:
        other = tile_at(second, second)
        parts.append(jnp.where(columns >= rows, tile_at(first, first), other))
        tails.append(jnp.sum(jnp.where(rows == columns, other, 0.0), axis=0, keepdims=True))
    tails.append(jnp.zeros((PACKED - TAIL - len(tails), TILE), jnp.float32))
    return parts + [jnp.concatenate(tails, axis=0)]


def unpack(packed, target):
    rows, columns = tile_indices()

    def store(r, c, value):
        target[r * TILE : (r + 1) * TILE, c * TILE : (c + 1) * TILE] = value.astype(target.dtype)

    for place, (r, c) in enumerate(UPPER):
        value = packed(place * TILE, TILE)
        store(r, c, value)
        store(c, r, value.T)
    tails = packed(TAIL, PACKED - TAIL)
    for place, (first, second) in enumerate(DIAGONAL):
        value = packed((len(UPPER) + place) * TILE, TILE)
        turned = value.T
        store(first, first, jnp.where(columns >= rows, value, turned))
        upper = jnp.where(columns > rows, turned, tails[place : place + 1, :])
        store(second, second, jnp.where(columns < rows, value, upper))


def store_parts(out, parts, extra=()):
    start = 0
    for part in parts:
        stop = start + part.shape[0]
        for other in extra:
            part = part + other[start:stop, :]
        out[start:stop, :] = part.astype(out.dtype)
        start = stop


def products_kernel(count, adds, *refs):
    pieces, extra = refs[:RING], refs[RING : RING + adds]
    outs, joined = refs[-1 - count : -1], refs[-1]
    tokens = pieces[0].shape[1]
    for index, out in enumerate(outs):
        for place, piece in enumerate(pieces):
            joined[:, place * tokens : (place + 1) * tokens] = piece[
                index * BLK : (index + 1) * BLK, :
            ]
        strips = [
            lax.dot_general(
                joined[r * TILE : (r + 1) * TILE, :],
                joined[r * TILE :, :],
                (((1,), (1,)), ((), ())),
                preferred_element_type=jnp.float32,
            )
            for r in range(SIDE)
        ]
        store_parts(out, pack(lambda r, c: strips[r][:, (c - r) * TILE : (c - r + 1) * TILE]), extra)


def products(pieces, *extra, after=()):
    tokens = pieces[0].shape[1]
    count = pieces[0].shape[0] // BLK
    return pl.pallas_call(
        functools.partial(products_kernel, count, len(extra)),
        out_shape=[jax.ShapeDtypeStruct((PACKED, TILE), jnp.float32)] * count,
        in_specs=[VMEM] * (RING + len(extra)) + [ANY] * len(after),
        out_specs=[VMEM] * count,
        scratch_shapes=[pltpu.VMEM((BLK, RING * tokens), jnp.bfloat16)],
        compiler_params=PARAMS,
        name="products",
    )(*pieces, *extra, *after)


def halves(value):
    high = value.astype(jnp.bfloat16)
    low = (value - high.astype(jnp.float32)).astype(jnp.bfloat16)
    return high, low


def dot(left, right):
    return jnp.dot(left, right, preferred_element_type=jnp.float32)


def dot3(left, right):
    left_high, left_low = left
    right_high, right_low = right
    return dot(left_high, right_high) + (dot(left_high, right_low) + dot(left_low, right_high))


def newton_kernel(total, own, sibling, far, out, damped):
    rows = lax.broadcasted_iota(jnp.int32, (BLK, BLK), 0)
    columns = lax.broadcasted_iota(jnp.int32, (BLK, BLK), 1)
    identity = jnp.where(rows == columns, 1.0, 0.0).astype(jnp.float32)
    def packed(start, size):
        part = slice(start, start + size)
        return (own[part, :] + sibling[part, :] + far[part, :]) / float(total)

    unpack(packed, damped)
    matrix = damped[...] + DAMPING * identity
    scale = 1.0 / jnp.max(jnp.sum(jnp.abs(matrix), axis=1, keepdims=True), axis=0, keepdims=True)
    matrix_parts = halves(matrix)
    approx = scale * (2.0 * identity - scale * matrix)

    def step(iteration, current):
        parts = halves(current)
        residual = identity - dot3(matrix_parts, parts)
        return current + dot3(parts, halves(residual))

    approx = lax.fori_loop(1, NS_STEPS, step, approx)
    store_parts(
        out,
        pack(lambda r, c: approx[r * TILE : (r + 1) * TILE, c * TILE : (c + 1) * TILE]),
    )


def newton(total, own, sibling, far):
    return pl.pallas_call(
        functools.partial(newton_kernel, total),
        out_shape=jax.ShapeDtypeStruct((PACKED, TILE), jnp.bfloat16),
        in_specs=[VMEM] * 3,
        out_specs=VMEM,
        scratch_shapes=[pltpu.VMEM((BLK, BLK), jnp.float32)],
        compiler_params=PARAMS,
        name="newton",
    )(own, sibling, far)


def apply_kernel(places, waits, *refs):
    count = len(places)
    inverses, pieces = refs[:count], refs[count : count + RING]
    outs, (full, joined) = refs[count + RING + waits : -2], refs[-2:]
    columns = pieces[0].shape[1]
    for index, (place, inverse) in enumerate(zip(places, inverses)):
        unpack(lambda start, size: inverse[start : start + size, :].astype(jnp.float32), full)
        for offset, piece in enumerate(pieces):
            joined[:, offset * columns : (offset + 1) * columns] = piece[
                place * BLK : (place + 1) * BLK, :
            ]
        result = dot(full[...], joined[...]).astype(jnp.bfloat16)
        for offset in range(RING):
            outs[offset][index * BLK : (index + 1) * BLK, :] = result[
                :, offset * columns : (offset + 1) * columns
            ]


def apply(places, inverses, pieces, after=()):
    columns = pieces[0].shape[1]
    shapes = [jax.ShapeDtypeStruct((len(places) * BLK, columns), jnp.bfloat16)] * RING
    return pl.pallas_call(
        functools.partial(apply_kernel, places, len(after)),
        out_shape=shapes,
        in_specs=[VMEM] * (RING + len(places)) + [ANY] * len(after),
        out_specs=[VMEM] * len(shapes),
        scratch_shapes=[
            pltpu.VMEM((BLK, BLK), jnp.bfloat16),
            pltpu.VMEM((BLK, RING * columns), jnp.bfloat16),
        ],
        compiler_params=PARAMS,
        name="apply",
    )(*inverses, *pieces, *after)


def put_back_kernel(groups, last, order, *refs):
    pieces, refs = refs[: RING * len(groups)], refs[RING * len(groups) :]
    if last:
        before, out, wide, held = refs
        wide[...] = before[...]
    else:
        wide, held = refs
    for group, places in enumerate(groups):
        for index, place in enumerate(places):
            for offset in range(RING):
                start = block_start(PHASES[place], offset)
                piece = pieces[group * RING + offset]
                held[...] = piece[index * BLK : (index + 1) * BLK, :].astype(jnp.float32)

                def step(batch, carry):
                    first = pl.multiple_of(batch * UNROLL, UNROLL)
                    for inner in range(UNROLL):
                        row = order[0, start + first + inner]
                        wide[pl.ds(row, 1), :] = held[pl.ds(first + inner, 1), :]
                    return carry

                lax.fori_loop(0, BLK // UNROLL, step, 0)
    if last:
        out[...] = wide[...].astype(jnp.bfloat16)


def put_back(order, groups, pieces, before=None):
    columns = pieces[0].shape[1]
    features = order.shape[1]
    last = before is not None
    wide = pltpu.VMEM((features, columns), jnp.float32)
    held = pltpu.VMEM((BLK, columns), jnp.float32)
    return pl.pallas_call(
        functools.partial(put_back_kernel, groups, last),
        out_shape=jax.ShapeDtypeStruct(
            (features, columns), jnp.bfloat16 if last else jnp.float32
        ),
        in_specs=[SMEM] + [VMEM] * (len(pieces) + last),
        out_specs=VMEM,
        scratch_shapes=[wide, held] if last else [held],
        compiler_params=PARAMS,
        name="put_back",
    )(order, *pieces, *([before] if last else []))


def exchange(pieces, sign):
    return [pieces[0]] + [ring_shift(pieces[k], sign * k) for k in range(1, RING)]


def shards(factor_rows, feature_order, gradients):
    rows = factor_rows[0]
    grads = gradients[0]
    total = rows.shape[0] * lax.axis_size("dp")

    order = feature_order
    picked_0 = pick_columns(PHASES[:1], order, rows)
    picked_1 = pick_columns(PHASES[1:2], order, rows, after=picked_0[:1])
    arrived_0 = exchange(picked_0, 1)
    arrived_1 = exchange(picked_1, 1)
    (partial_0,) = products(arrived_0, after=picked_1[:1])
    from_3 = line_swap(partial_0, 1)
    picked_2 = pick_columns(PHASES[2:3], order, rows, after=[partial_0])
    (partial_1,) = products(arrived_1, from_3, after=picked_2[:1])
    from_2 = line_swap(partial_1, 2)
    arrived_2 = exchange(picked_2, 1)
    picked_3 = pick_columns(PHASES[3:], order, rows, after=[partial_1])
    (partial_2,) = products(arrived_2, after=picked_3[:1])
    partial_2, picked_3 = lax.optimization_barrier((partial_2, picked_3))
    from_1 = line_swap(partial_2, 1)
    arrived_3 = exchange(picked_3, 1)
    grad_pieces = pick_grads(order, grads, after=[partial_2])
    (partial_3,) = products(arrived_3, after=grad_pieces[:1])
    partial_3, grad_pieces = lax.optimization_barrier((partial_3, grad_pieces))
    arrived_grads = exchange(grad_pieces, 1)
    inverse = newton(total, partial_3, from_1, from_2)

    inverse_1, inverse_2, inverse_3 = [line_swap(inverse, mask) for mask in (1, 2, 3)]
    made_a = apply((3, 2), [inverse, inverse_1], arrived_grads)
    result_a = exchange(made_a, -1)
    made_b = apply((1, 0), [inverse_2, inverse_3], arrived_grads, after=result_a[1:2])
    result_b = exchange(made_b, -1)
    partly = put_back(order, ((3, 2),), result_a)
    return put_back(order, ((1, 0),), result_b, partly)[None]


def solution(mesh):
    return jax.shard_map(
        shards,
        mesh=mesh,
        in_specs=(
            P("owner", ("member", "dp"), None),
            P("owner", None),
            P("owner", None, ("member", "dp")),
        ),
        out_specs=P("owner", None, ("member", "dp")),
        check_vma=False,
    )
```

time: 452 us -> 150 us (0.33)
  waiting for transfers between devices: 261 us -> 42.2 us
  local copies, waits for them, and re-layouts: 108 us -> 2.96 us
  Pallas kernels: 0 us -> 67 us
  matrix products: 62 us -> 0 us
  starting transfers between devices: 0.04 us -> 37.8 us
  between operations: 14.2 us -> 0.17 us
  other arithmetic: 4.81 us -> 0 us
    reduce_scatter x1 -> x0, waiting for transfers between devices: 191 us -> none  [shards(): lax.psum_scatter(product.reshape(owned_count * BLK * lax.axis_size('dp'),...]
    all_gather x1 -> x0, waiting for transfers between devices: 69.9 us -> none  [shards(): lax.all_gather(inverse, 'dp', axis=0, tiled=True)]
    pallas_call x0 -> x14, Pallas kernels: none -> 67 us  [the longest x1 22.7 us: newton(): pl.pallas_call(functools.partial(newton_kernel, total), out_shape=jax.Sha...]
    gather x2 -> x0, local copies, waits for them, and re-layouts: 63.1 us -> none  [the longest x1 33.6 us: shards(): jnp.take(data_rows, feature_perm, axis=1)]
    dot_general x26 -> x0, matrix products: 62 us -> none  [the longest x12 22.3 us: newton_step(): jnp.einsum('kij,kjl->kil', damped, current, precision=lax.Precision.HIGHEST)]
    ppermute x0 -> x27, waiting for transfers between devices: none -> 42.2 us  [the longest x21 23.2 us: ring_shift(): return lax.ppermute(value, 'dp', pairs)]
    ppermute x0 -> x27, starting transfers between devices: none -> 37.8 us  [the longest x21 28.7 us: ring_shift(): return lax.ppermute(value, 'dp', pairs)]
    scatter x1 -> x0, local copies, waits for them, and re-layouts: 22.8 us -> none  [shards(): restored = jnp.zeros((feature_count, grad_rows.shape[1]), jnp.bfloat16).a...]
  transfers between devices with their start and end apart: 2 -> 27, of which waited for: 2 -> 12; matrix products, arithmetic and copies ran while one was open for 7% -> 0% of each run, Pallas kernels for 0% -> 37%
where the time goes in v1:
time: 150 us
  Pallas kernels  67 us (45%)
  waiting for transfers between devices  42.2 us (28%)
  starting transfers between devices  37.8 us (25%)
  local copies, waits for them, and re-layouts  2.96 us (2%)
    ppermute x21, starting transfers between devices, ring_shift(): return lax.ppermute(value, 'dp', pairs)  28.7 us
    ppermute x21, waiting for transfers between devices, ring_shift(): return lax.ppermute(value, 'dp', pairs)  23.2 us
    pallas_call x1, Pallas kernels, newton(): pl.pallas_call(functools.partial(newton_kernel, total), out_shape=jax.Sha...  22.7 us
    ppermute x6, waiting for transfers between devices, line_swap(): return lax.ppermute(value, 'dp', pairs)  19 us
    pallas_call x4, Pallas kernels, pick_columns(): pl.pallas_call(functools.partial(pick_columns_kernel, phases), out_shape=...  19 us
    pallas_call x2, Pallas kernels, put_back(): pl.pallas_call(functools.partial(put_back_kernel, groups, last), out_shap...  11.2 us
    ppermute x6, starting transfers between devices, line_swap(): return lax.ppermute(value, 'dp', pairs)  9.11 us
    pallas_call x1, Pallas kernels, pick_grads(): pl.pallas_call(pick_grads_kernel, out_shape=[jax.ShapeDtypeStruct((LINE *...  8.59 us
  transfers between devices with their start and end apart: 27, of which 12 were waited for; matrix products, arithmetic and copies ran while one was open for 0% of the time, Pallas kernels for 37%

profile of v1, /device:TPU:1, one launch (start us, length us, event | category | flops | bytes accessed | tf_op | source)
XLA Modules:
  0.0 150.1 jit_solution(8763409539811160090)
XLA Ops:
  0.0 2.2 %copy-done = bf16[1,256,8192]{2,1,0:T(8,128)(2,1)S(1)} copy-done((bf16[1,256,8192]{2,1,0:T(8,128)(2,1)S(1)}, bf16[1,256,8192]{2,1,0:T(8,128)(2,1)}, u32[]{:S(2)}) %copy-start) | copy-done | bytes 4194328
  2.9 4.7 %pick_columns.4 = (bf16[512,256]{1,0:T(8,128)(2,1)S(1)}, bf16[512,256]{1,0:T(8,128)(2,1)S(1)}, bf16[512,256]{1,0:T(8,128)(2,1)S(1)}, bf16[512,256]{1,0:T(8,128)(2,1)S(1)}) custom-call(s32[1,8192]{1,0:T(1,128)S(1)} %copy-done.3, bf16[256,8192]{1,0:T(8,128)(2,1)S(1)} %bitcast.3), custom_call_target="tpu_custom_call" | custom-call | tf_op jit(solution)/shard_map/pick_columns/pallas_call | solution.py:81
  7.7 2.1 %collective-permute-start = (bf16[512,256]{1,0:T(8,128)(2,1)S(1)}, bf16[512,256]{1,0:T(8,128)(2,1)S(1)}, u32[]{:S(2)}, u32[]{:S(2)}) collective-permute-start(bf16[512,256]{1,0:T(8,128)(2,1)S(1)} %get-tuple-element.44), channel_id=1, source_target_pairs={{0,2},{2,4},{4,6},{6,0},{8,10},{10,12},{12,14},{14,8},{16,18},{18,... | collective-permute-start | bytes 786440 | tf_op jit(solution)/shard_map/ppermute | solution.py:35
  9.8 2.5 %collective-permute-start.1 = (bf16[512,256]{1,0:T(8,128)(2,1)S(1)}, bf16[512,256]{1,0:T(8,128)(2,1)S(1)}, u32[]{:S(2)}, u32[]{:S(2)}) collective-permute-start(bf16[512,256]{1,0:T(8,128)(2,1)S(1)} %get-tuple-element.45), channel_id=1, source_target_pairs={{0,4},{2,6},{4,0},{6,2},{8,12},{10,14},{12,8},{14,10},{16,20},{18,... | collective-permute-start | bytes 786440 | tf_op jit(solution)/shard_map/ppermute | solution.py:35
  13.4 4.7 %pick_columns.5 = (bf16[512,256]{1,0:T(8,128)(2,1)S(1)}, bf16[512,256]{1,0:T(8,128)(2,1)S(1)}, bf16[512,256]{1,0:T(8,128)(2,1)S(1)}, bf16[512,256]{1,0:T(8,128)(2,1)S(1)}) custom-call(s32[1,8192]{1,0:T(1,128)S(1)} %copy-done.3, bf16[256,8192]{1,0:T(8,128)(2,1)S(1)} %bitcast.4, bf16[512,256]{1,0:T(8,128)(2,1)S(1)} %get-tuple-element.43.refs_0_), custom_call_target="tpu_custom_call" | custom-call | tf_op jit(solution)/shard_map/pick_columns/pallas_call | solution.py:81
  18.2 5.4 %collective-permute-done.1.refs_2_ = bf16[512,256]{1,0:T(8,128)(2,1)S(1)} collective-permute-done((bf16[512,256]{1,0:T(8,128)(2,1)S(1)}, bf16[512,256]{1,0:T(8,128)(2,1)S(1)}, u32[]{:S(2)}, u32[]{:S(2)}) %collective-permute-start.1) | collective-permute-done | bytes 262176 | tf_op jit(solution)/shard_map/ppermute | solution.py:35
  24.5 1.7 %collective-permute-start.9 = (f32[1040,128]{1,0:T(8,128)S(1)}, f32[1040,128]{1,0:T(8,128)S(1)}, u32[]{:S(2)}, u32[]{:S(2)}) collective-permute-start(f32[1040,128]{1,0:T(8,128)S(1)} %products.4.refs_0_), channel_id=1, source_target_pairs={{0,8},{2,10},{4,12},{6,14},{8,0},{10,2},{12,4},{14,6},{16,24},{18,... | collective-permute-start | bytes 1597448 | tf_op jit(solution)/shard_map/ppermute | solution.py:40
  26.3 1.4 collective-permute-start.6
  27.6 2.8 %collective-permute-start.7 = (bf16[512,256]{1,0:T(8,128)(2,1)S(1)}, bf16[512,256]{1,0:T(8,128)(2,1)S(1)}, u32[]{:S(2)}, u32[]{:S(2)}) collective-permute-start(bf16[512,256]{1,0:T(8,128)(2,1)S(1)} %get-tuple-element.53), channel_id=1, source_target_pairs={{0,4},{2,6},{4,0},{6,2},{8,12},{10,14},{12,8},{14,10},{16,20},{18,... | collective-permute-start | bytes 786440 | tf_op jit(solution)/shard_map/ppermute | solution.py:35
  30.5 4.7 %pick_columns.6 = (bf16[512,256]{1,0:T(8,128)(2,1)S(1)}, bf16[512,256]{1,0:T(8,128)(2,1)S(1)}, bf16[512,256]{1,0:T(8,128)(2,1)S(1)}, bf16[512,256]{1,0:T(8,128)(2,1)S(1)}) custom-call(s32[1,8192]{1,0:T(1,128)S(1)} %copy-done.4, bf16[256,8192]{1,0:T(8,128)(2,1)S(1)} %bitcast.5, f32[1040,128]{1,0:T(8,128)S(1)} %products.4.refs_0_), custom_call_target="tpu_custom_call" | custom-call | tf_op jit(solution)/shard_map/pick_columns/pallas_call | solution.py:81
  35.3 1.5 %collective-permute-start.3 = (bf16[512,256]{1,0:T(8,128)(2,1)S(1)}, bf16[512,256]{1,0:T(8,128)(2,1)S(1)}, u32[]{:S(2)}, u32[]{:S(2)}) collective-permute-start(bf16[512,256]{1,0:T(8,128)(2,1)S(1)} %get-tuple-element.49), channel_id=1, source_target_pairs={{0,2},{2,4},{4,6},{6,0},{8,10},{10,12},{12,14},{14,8},{16,18},{18,... | collective-permute-start | bytes 786440 | tf_op jit(solution)/shard_map/ppermute | solution.py:35
  36.9 4.8 %collective-permute-done.7.refs_2_ = bf16[512,256]{1,0:T(8,128)(2,1)S(1)} collective-permute-done((bf16[512,256]{1,0:T(8,128)(2,1)S(1)}, bf16[512,256]{1,0:T(8,128)(2,1)S(1)}, u32[]{:S(2)}, u32[]{:S(2)}) %collective-permute-start.7) | collective-permute-done | bytes 262176 | tf_op jit(solution)/shard_map/ppermute | solution.py:35
  43.4 3.1 %collective-permute-start.14 = (f32[1040,128]{1,0:T(8,128)S(1)}, f32[1040,128]{1,0:T(8,128)S(1)}, u32[]{:S(2)}, u32[]{:S(2)}) collective-permute-start(f32[1040,128]{1,0:T(8,128)S(1)} %products.5.refs_0_), channel_id=1, source_target_pairs={{0,16},{2,18},{4,20},{6,22},{8,24},{10,26},{12,28},{14,30},{16,0},... | collective-permute-start | bytes 1597448 | tf_op jit(solution)/shard_map/ppermute | solution.py:40
  46.4 4.7 %pick_columns.7 = (bf16[512,256]{1,0:T(8,128)(2,1)S(1)}, bf16[512,256]{1,0:T(8,128)(2,1)S(1)}, bf16[512,256]{1,0:T(8,128)(2,1)S(1)}, bf16[512,256]{1,0:T(8,128)(2,1)S(1)}) custom-call(s32[1,8192]{1,0:T(1,128)S(1)} %copy-done.4, bf16[256,8192]{1,0:T(8,128)(2,1)S(1)} %bitcast.6, f32[1040,128]{1,0:T(8,128)S(1)} %products.5.refs_0_), custom_call_target="tpu_custom_call" | custom-call | tf_op jit(solution)/shard_map/pick_columns/pallas_call | solution.py:81
  51.2 1.8 %collective-permute-done.4.refs_2_ = bf16[512,256]{1,0:T(8,128)(2,1)S(1)} collective-permute-done((bf16[512,256]{1,0:T(8,128)(2,1)S(1)}, bf16[512,256]{1,0:T(8,128)(2,1)S(1)}, u32[]{:S(2)}, u32[]{:S(2)}) %collective-permute-start.4) | collective-permute-done | bytes 262176 | tf_op jit(solution)/shard_map/ppermute | solution.py:35
  55.7 2.5 %collective-permute-start.11 = (bf16[512,256]{1,0:T(8,128)(2,1)S(1)}, bf16[512,256]{1,0:T(8,128)(2,1)S(1)}, u32[]{:S(2)}, u32[]{:S(2)}) collective-permute-start(bf16[512,256]{1,0:T(8,128)(2,1)S(1)} %get-tuple-element.61), channel_id=1, source_target_pairs={{0,4},{2,6},{4,0},{6,2},{8,12},{10,14},{12,8},{14,10},{16,20},{18,... | collective-permute-start | bytes 786440 | tf_op jit(solution)/shard_map/ppermute | solution.py:35
  58.2 8.6 %pick_grads.1 = (bf16[2048,128]{1,0:T(8,128)(2,1)S(1)}, bf16[2048,128]{1,0:T(8,128)(2,1)S(1)}, bf16[2048,128]{1,0:T(8,128)(2,1)S(1)}, bf16[2048,128]{1,0:T(8,128)(2,1)S(1)}) custom-call(s32[1,8192]{1,0:T(1,128)S(1)} %copy-done.4, bf16[8192,128]{1,0:T(8,128)(2,1)S(1)} %bitcast.7, f32[1040,128]{1,0:T(8,128)S(1)} %products.6.refs_0_), custom_call_target="tpu_custom_call" | custom-call | tf_op jit(solution)/shard_map/pick_grads/pallas_call | solution.py:104
  69.5 2.7 %collective-permute-start.17 = (bf16[2048,128]{1,0:T(8,128)(2,1)S(1)}, bf16[2048,128]{1,0:T(8,128)(2,1)S(1)}, u32[]{:S(2)}, u32[]{:S(2)}) collective-permute-start(bf16[2048,128]{1,0:T(8,128)(2,1)S(1)} %get-tuple-element.70), channel_id=1, source_target_pairs={{0,2},{2,4},{4,6},{6,0},{8,10},{10,12},{12,14},{14,8},{16,18},{18,... | collective-permute-start | bytes 1572872 | tf_op jit(solution)/shard_map/ppermute | solution.py:35
  72.1 2.0 %collective-permute-start.18 = (bf16[2048,128]{1,0:T(8,128)(2,1)S(1)}, bf16[2048,128]{1,0:T(8,128)(2,1)S(1)}, u32[]{:S(2)}, u32[]{:S(2)}) collective-permute-start(bf16[2048,128]{1,0:T(8,128)(2,1)S(1)} %get-tuple-element.71), channel_id=1, source_target_pairs={{0,4},{2,6},{4,0},{6,2},{8,12},{10,14},{12,8},{14,10},{16,20},{18,... | collective-permute-start | bytes 1572872 | tf_op jit(solution)/shard_map/ppermute | solution.py:35
  74.6 2.6 %collective-permute-done.13.sibling = f32[1040,128]{1,0:T(8,128)S(1)} collective-permute-done((f32[1040,128]{1,0:T(8,128)S(1)}, f32[1040,128]{1,0:T(8,128)S(1)}, u32[]{:S(2)}, u32[]{:S(2)}) %collective-permute-start.13) | collective-permute-done | bytes 532512 | tf_op jit(solution)/shard_map/ppermute | solution.py:40
  77.2 22.7 %newton.1.refs_0_ = bf16[1040,128]{1,0:T(8,128)(2,1)S(1)} custom-call(f32[1040,128]{1,0:T(8,128)S(1)} %products.7.own, f32[1040,128]{1,0:T(8,128)S(1)} %collective-permute-done.13.sibling, f32[1040,128]{1,0:T(8,128)S(1)} %collective-permute-done.14.far), custom_call_target="tpu_custom_call" | custom-call | tf_op jit(solution)/shard_map/newton/pallas_call | solution.py:243
  100.3 3.3 %collective-permute-start.16 = (bf16[1040,128]{1,0:T(8,128)(2,1)S(1)}, bf16[1040,128]{1,0:T(8,128)(2,1)S(1)}, u32[]{:S(2)}, u32[]{:S(2)}) collective-permute-start(bf16[1040,128]{1,0:T(8,128)(2,1)S(1)} %newton.1.refs_0_), channel_id=1, source_target_pairs={{0,24},{2,26},{4,28},{6,30},{8,16},{10,18},{12,20},{14,22},{16,8},... | collective-permute-start | bytes 798728 | tf_op jit(solution)/shard_map/ppermute | solution.py:40
  103.8 1.7 %collective-permute-done.20.refs_1_ = bf16[1040,128]{1,0:T(8,128)(2,1)S(1)} collective-permute-done((bf16[1040,128]{1,0:T(8,128)(2,1)S(1)}, bf16[1040,128]{1,0:T(8,128)(2,1)S(1)}, u32[]{:S(2)}, u32[]{:S(2)}) %collective-permute-start.20) | collective-permute-done | bytes 266272 | tf_op jit(solution)/shard_map/ppermute | solution.py:40
  106.4 1.7 %collective-permute-start.21 = (bf16[1024,128]{1,0:T(8,128)(2,1)S(1)}, bf16[1024,128]{1,0:T(8,128)(2,1)S(1)}, u32[]{:S(2)}, u32[]{:S(2)}) collective-permute-start(bf16[1024,128]{1,0:T(8,128)(2,1)S(1)} %get-tuple-element.73), channel_id=1, source_target_pairs={{0,6},{2,0},{4,2},{6,4},{8,14},{10,8},{12,10},{14,12},{16,22},{18,... | collective-permute-start | bytes 786440 | tf_op jit(solution)/shard_map/ppermute | solution.py:35
  108.1 2.5 %collective-permute-start.25 = (bf16[1024,128]{1,0:T(8,128)(2,1)S(1)}, bf16[1024,128]{1,0:T(8,128)(2,1)S(1)}, u32[]{:S(2)}, u32[]{:S(2)}) collective-permute-start(bf16[1024,128]{1,0:T(8,128)(2,1)S(1)} %get-tuple-element.79), channel_id=1, source_target_pairs={{0,4},{2,6},{4,0},{6,2},{8,12},{10,14},{12,8},{14,10},{16,20},{18,... | collective-permute-start | bytes 786440 | tf_op jit(solution)/shard_map/ppermute | solution.py:35
  110.6 3.9 %collective-permute-done.16.refs_1_ = bf16[1040,128]{1,0:T(8,128)(2,1)S(1)} collective-permute-done((bf16[1040,128]{1,0:T(8,128)(2,1)S(1)}, bf16[1040,128]{1,0:T(8,128)(2,1)S(1)}, u32[]{:S(2)}, u32[]{:S(2)}) %collective-permute-start.16) | collective-permute-done | bytes 266272 | tf_op jit(solution)/shard_map/ppermute | solution.py:40
  114.5 10.7 %collective-permute-done.15.refs_0_ = bf16[1040,128]{1,0:T(8,128)(2,1)S(1)} collective-permute-done((bf16[1040,128]{1,0:T(8,128)(2,1)S(1)}, bf16[1040,128]{1,0:T(8,128)(2,1)S(1)}, u32[]{:S(2)}, u32[]{:S(2)}) %collective-permute-start.15) | collective-permute-done | bytes 266272 | tf_op jit(solution)/shard_map/ppermute | solution.py:40
  126.2 3.3 %collective-permute-start.22 = (bf16[1024,128]{1,0:T(8,128)(2,1)S(1)}, bf16[1024,128]{1,0:T(8,128)(2,1)S(1)}, u32[]{:S(2)}, u32[]{:S(2)}) collective-permute-start(bf16[1024,128]{1,0:T(8,128)(2,1)S(1)} %get-tuple-element.75), channel_id=1, source_target_pairs={{0,6},{2,0},{4,2},{6,4},{8,14},{10,8},{12,10},{14,12},{16,22},{18,... | collective-permute-start | bytes 786440 | tf_op jit(solution)/shard_map/ppermute | solution.py:35
  130.1 4.7 %put_back.2.refs_4_ = f32[8192,128]{1,0:T(8,128)S(1)} custom-call(s32[1,8192]{1,0:T(1,128)S(1)} %copy-done.4, bf16[1024,128]{1,0:T(8,128)(2,1)S(1)} %get-tuple-element.78.refs_0_, bf16[1024,128]{1,0:T(8,128)(2,1)S(1)} %collective-permute-done.21.refs_6_.refs_1_, bf16[1024,128]{1,0:T(8,128)(2,1)S(1)} %collective-permute-done.25.refs_2_, ...), custom_call_target="tpu_custom_call" | custom-call | tf_op jit(solution)/shard_map/put_back/pallas_call | solution.py:321
  134.9 1.7 %collective-permute-done.22.refs_1_ = bf16[1024,128]{1,0:T(8,128)(2,1)S(1)} collective-permute-done((bf16[1024,128]{1,0:T(8,128)(2,1)S(1)}, bf16[1024,128]{1,0:T(8,128)(2,1)S(1)}, u32[]{:S(2)}, u32[]{:S(2)}) %collective-permute-start.22) | collective-permute-done | bytes 262176 | tf_op jit(solution)/shard_map/ppermute | solution.py:35
  136.6 7.1 %collective-permute-done.24.refs_3_ = bf16[1024,128]{1,0:T(8,128)(2,1)S(1)} collective-permute-done((bf16[1024,128]{1,0:T(8,128)(2,1)S(1)}, bf16[1024,128]{1,0:T(8,128)(2,1)S(1)}, u32[]{:S(2)}, u32[]{:S(2)}) %collective-permute-start.24) | collective-permute-done | bytes 262176 | tf_op jit(solution)/shard_map/ppermute | solution.py:35
  143.6 6.5 %put_back.3 = bf16[8192,128]{1,0:T(8,128)(2,1)} custom-call(s32[1,8192]{1,0:T(1,128)S(1)} %copy-done.4, bf16[1024,128]{1,0:T(8,128)(2,1)S(1)} %get-tuple-element.74.refs_0_, bf16[1024,128]{1,0:T(8,128)(2,1)S(1)} %collective-permute-done.22.refs_1_, bf16[1024,128]{1,0:T(8,128)(2,1)S(1)} %collective-permute-done.23.refs_2_, ...), custom_call_target="tpu_custom_call" | custom-call | tf_op jit(solution)/shard_map/put_back/pallas_call | solution.py:321
  (46 shorter events, 13.5 us)
Async XLA Ops:
  0.0 2.2 %copy-start = (bf16[1,256,8192]{2,1,0:T(8,128)(2,1)S(1)}, bf16[1,256,8192]{2,1,0:T(8,128)(2,1)}, u32[]{:S(2)}) copy-start(bf16[1,256,8192]{2,1,0:T(8,128)(2,1)} %param.3) | copy-start | bytes 12582916
  2.2 0.8 copy-start.3
  7.7 22.8 %copy-start.1 = (bf16[1,256,8192]{2,1,0:T(8,128)(2,1)S(1)}, bf16[1,256,8192]{2,1,0:T(8,128)(2,1)}, u32[]{:S(2)}) copy-start(bf16[1,256,8192]{2,1,0:T(8,128)(2,1)} %param.3) | copy-start | bytes 12582916
  7.7 22.8 %copy-start.4 = (s32[1,8192]{1,0:T(1,128)S(1)}, s32[1,8192]{1,0:T(1,128)}, u32[]{:S(2)}) copy-start(s32[1,8192]{1,0:T(1,128)} %order.13) | copy-start | bytes 98308
  7.7 10.5 %collective-permute-start = (bf16[512,256]{1,0:T(8,128)(2,1)S(1)}, bf16[512,256]{1,0:T(8,128)(2,1)S(1)}, u32[]{:S(2)}, u32[]{:S(2)}) collective-permute-start(bf16[512,256]{1,0:T(8,128)(2,1)S(1)} %get-tuple-element.44), channel_id=1, source_target_pairs={{0,2},{2,4},{4,6},{6,0},{8,10},{10,12},{12,14},{14,8},{16,18},{18,... | collective-permute-start | bytes 786440 | tf_op jit(solution)/shard_map/ppermute | solution.py:35
  9.8 13.8 %collective-permute-start.1 = (bf16[512,256]{1,0:T(8,128)(2,1)S(1)}, bf16[512,256]{1,0:T(8,128)(2,1)S(1)}, u32[]{:S(2)}, u32[]{:S(2)}) collective-permute-start(bf16[512,256]{1,0:T(8,128)(2,1)S(1)} %get-tuple-element.45), channel_id=1, source_target_pairs={{0,4},{2,6},{4,0},{6,2},{8,12},{10,14},{12,8},{14,10},{16,20},{18,... | collective-permute-start | bytes 786440 | tf_op jit(solution)/shard_map/ppermute | solution.py:35
  12.3 11.3 %collective-permute-start.2 = (bf16[512,256]{1,0:T(8,128)(2,1)S(1)}, bf16[512,256]{1,0:T(8,128)(2,1)S(1)}, u32[]{:S(2)}, u32[]{:S(2)}) collective-permute-start(bf16[512,256]{1,0:T(8,128)(2,1)S(1)} %get-tuple-element.46), channel_id=1, source_target_pairs={{0,6},{2,0},{4,2},{6,4},{8,14},{10,8},{12,10},{14,12},{16,22},{18,... | collective-permute-start | bytes 786440 | tf_op jit(solution)/shard_map/ppermute | solution.py:35
  24.5 17.9 %collective-permute-start.9 = (f32[1040,128]{1,0:T(8,128)S(1)}, f32[1040,128]{1,0:T(8,128)S(1)}, u32[]{:S(2)}, u32[]{:S(2)}) collective-permute-start(f32[1040,128]{1,0:T(8,128)S(1)} %products.4.refs_0_), channel_id=1, source_target_pairs={{0,8},{2,10},{4,12},{6,14},{8,0},{10,2},{12,4},{14,6},{16,24},{18,... | collective-permute-start | bytes 1597448 | tf_op jit(solution)/shard_map/ppermute | solution.py:40
  26.3 10.5 %collective-permute-start.6 = (bf16[512,256]{1,0:T(8,128)(2,1)S(1)}, bf16[512,256]{1,0:T(8,128)(2,1)S(1)}, u32[]{:S(2)}, u32[]{:S(2)}) collective-permute-start(bf16[512,256]{1,0:T(8,128)(2,1)S(1)} %get-tuple-element.52), channel_id=1, source_target_pairs={{0,2},{2,4},{4,6},{6,0},{8,10},{10,12},{12,14},{14,8},{16,18},{18,... | collective-permute-start | bytes 786440 | tf_op jit(solution)/shard_map/ppermute | solution.py:35
  27.6 14.1 %collective-permute-start.7 = (bf16[512,256]{1,0:T(8,128)(2,1)S(1)}, bf16[512,256]{1,0:T(8,128)(2,1)S(1)}, u32[]{:S(2)}, u32[]{:S(2)}) collective-permute-start(bf16[512,256]{1,0:T(8,128)(2,1)S(1)} %get-tuple-element.53), channel_id=1, source_target_pairs={{0,4},{2,6},{4,0},{6,2},{8,12},{10,14},{12,8},{14,10},{16,20},{18,... | collective-permute-start | bytes 786440 | tf_op jit(solution)/shard_map/ppermute | solution.py:35
  30.5 11.9 %collective-permute-start.8 = (bf16[512,256]{1,0:T(8,128)(2,1)S(1)}, bf16[512,256]{1,0:T(8,128)(2,1)S(1)}, u32[]{:S(2)}, u32[]{:S(2)}) collective-permute-start(bf16[512,256]{1,0:T(8,128)(2,1)S(1)} %get-tuple-element.54), channel_id=1, source_target_pairs={{0,6},{2,0},{4,2},{6,4},{8,14},{10,8},{12,10},{14,12},{16,22},{18,... | collective-permute-start | bytes 786440 | tf_op jit(solution)/shard_map/ppermute | solution.py:35
  35.3 15.9 %collective-permute-start.3 = (bf16[512,256]{1,0:T(8,128)(2,1)S(1)}, bf16[512,256]{1,0:T(8,128)(2,1)S(1)}, u32[]{:S(2)}, u32[]{:S(2)}) collective-permute-start(bf16[512,256]{1,0:T(8,128)(2,1)S(1)} %get-tuple-element.49), channel_id=1, source_target_pairs={{0,2},{2,4},{4,6},{6,0},{8,10},{10,12},{12,14},{14,8},{16,18},{18,... | collective-permute-start | bytes 786440 | tf_op jit(solution)/shard_map/ppermute | solution.py:35
  36.8 16.2 %collective-permute-start.4 = (bf16[512,256]{1,0:T(8,128)(2,1)S(1)}, bf16[512,256]{1,0:T(8,128)(2,1)S(1)}, u32[]{:S(2)}, u32[]{:S(2)}) collective-permute-start(bf16[512,256]{1,0:T(8,128)(2,1)S(1)} %get-tuple-element.50), channel_id=1, source_target_pairs={{0,4},{2,6},{4,0},{6,2},{8,12},{10,14},{12,8},{14,10},{16,20},{18,... | collective-permute-start | bytes 786440 | tf_op jit(solution)/shard_map/ppermute | solution.py:35
  41.7 11.2 %collective-permute-start.5 = (bf16[512,256]{1,0:T(8,128)(2,1)S(1)}, bf16[512,256]{1,0:T(8,128)(2,1)S(1)}, u32[]{:S(2)}, u32[]{:S(2)}) collective-permute-start(bf16[512,256]{1,0:T(8,128)(2,1)S(1)} %get-tuple-element.51), channel_id=1, source_target_pairs={{0,6},{2,0},{4,2},{6,4},{8,14},{10,8},{12,10},{14,12},{16,22},{18,... | collective-permute-start | bytes 786440 | tf_op jit(solution)/shard_map/ppermute | solution.py:35
  42.4 15.8 %copy-start.2 = (bf16[1,8192,128]{2,1,0:T(8,128)(2,1)S(1)}, bf16[1,8192,128]{2,1,0:T(8,128)(2,1)}, u32[]{:S(2)}) copy-start(bf16[1,8192,128]{2,1,0:T(8,128)(2,1)} %param.5) | copy-start | bytes 6291460
  43.4 31.3 %collective-permute-start.14 = (f32[1040,128]{1,0:T(8,128)S(1)}, f32[1040,128]{1,0:T(8,128)S(1)}, u32[]{:S(2)}, u32[]{:S(2)}) collective-permute-start(f32[1040,128]{1,0:T(8,128)S(1)} %products.5.refs_0_), channel_id=1, source_target_pairs={{0,16},{2,18},{4,20},{6,22},{8,24},{10,26},{12,28},{14,30},{16,0},... | collective-permute-start | bytes 1597448 | tf_op jit(solution)/shard_map/ppermute | solution.py:40
  53.9 23.3 %collective-permute-start.13 = (f32[1040,128]{1,0:T(8,128)S(1)}, f32[1040,128]{1,0:T(8,128)S(1)}, u32[]{:S(2)}, u32[]{:S(2)}) collective-permute-start(f32[1040,128]{1,0:T(8,128)S(1)} %products.6.refs_0_), channel_id=1, source_target_pairs={{0,8},{2,10},{4,12},{6,14},{8,0},{10,2},{12,4},{14,6},{16,24},{18,... | collective-permute-start | bytes 1597448 | tf_op jit(solution)/shard_map/ppermute | solution.py:40
  54.4 12.4 %collective-permute-start.10 = (bf16[512,256]{1,0:T(8,128)(2,1)S(1)}, bf16[512,256]{1,0:T(8,128)(2,1)S(1)}, u32[]{:S(2)}, u32[]{:S(2)}) collective-permute-start(bf16[512,256]{1,0:T(8,128)(2,1)S(1)} %get-tuple-element.60), channel_id=1, source_target_pairs={{0,2},{2,4},{4,6},{6,0},{8,10},{10,12},{12,14},{14,8},{16,18},{18,... | collective-permute-start | bytes 786440 | tf_op jit(solution)/shard_map/ppermute | solution.py:35
  55.7 12.2 %collective-permute-start.11 = (bf16[512,256]{1,0:T(8,128)(2,1)S(1)}, bf16[512,256]{1,0:T(8,128)(2,1)S(1)}, u32[]{:S(2)}, u32[]{:S(2)}) collective-permute-start(bf16[512,256]{1,0:T(8,128)(2,1)S(1)} %get-tuple-element.61), channel_id=1, source_target_pairs={{0,4},{2,6},{4,0},{6,2},{8,12},{10,14},{12,8},{14,10},{16,20},{18,... | collective-permute-start | bytes 786440 | tf_op jit(solution)/shard_map/ppermute | solution.py:35
  58.2 10.4 %collective-permute-start.12 = (bf16[512,256]{1,0:T(8,128)(2,1)S(1)}, bf16[512,256]{1,0:T(8,128)(2,1)S(1)}, u32[]{:S(2)}, u32[]{:S(2)}) collective-permute-start(bf16[512,256]{1,0:T(8,128)(2,1)S(1)} %get-tuple-element.62), channel_id=1, source_target_pairs={{0,6},{2,0},{4,2},{6,4},{8,14},{10,8},{12,10},{14,12},{16,22},{18,... | collective-permute-start | bytes 786440 | tf_op jit(solution)/shard_map/ppermute | solution.py:35
  69.5 34.1 %collective-permute-start.17 = (bf16[2048,128]{1,0:T(8,128)(2,1)S(1)}, bf16[2048,128]{1,0:T(8,128)(2,1)S(1)}, u32[]{:S(2)}, u32[]{:S(2)}) collective-permute-start(bf16[2048,128]{1,0:T(8,128)(2,1)S(1)} %get-tuple-element.70), channel_id=1, source_target_pairs={{0,2},{2,4},{4,6},{6,0},{8,10},{10,12},{12,14},{14,8},{16,18},{18,... | collective-permute-start | bytes 1572872 | tf_op jit(solution)/shard_map/ppermute | solution.py:35
  72.1 31.6 %collective-permute-start.18 = (bf16[2048,128]{1,0:T(8,128)(2,1)S(1)}, bf16[2048,128]{1,0:T(8,128)(2,1)S(1)}, u32[]{:S(2)}, u32[]{:S(2)}) collective-permute-start(bf16[2048,128]{1,0:T(8,128)(2,1)S(1)} %get-tuple-element.71), channel_id=1, source_target_pairs={{0,4},{2,6},{4,0},{6,2},{8,12},{10,14},{12,8},{14,10},{16,20},{18,... | collective-permute-start | bytes 1572872 | tf_op jit(solution)/shard_map/ppermute | solution.py:35
  74.1 29.6 %collective-permute-start.19 = (bf16[2048,128]{1,0:T(8,128)(2,1)S(1)}, bf16[2048,128]{1,0:T(8,128)(2,1)S(1)}, u32[]{:S(2)}, u32[]{:S(2)}) collective-permute-start(bf16[2048,128]{1,0:T(8,128)(2,1)S(1)} %get-tuple-element.72), channel_id=1, source_target_pairs={{0,6},{2,0},{4,2},{6,4},{8,14},{10,8},{12,10},{14,12},{16,22},{18,... | collective-permute-start | bytes 1572872 | tf_op jit(solution)/shard_map/ppermute | solution.py:35
  99.9 5.6 %collective-permute-start.20 = (bf16[1040,128]{1,0:T(8,128)(2,1)S(1)}, bf16[1040,128]{1,0:T(8,128)(2,1)S(1)}, u32[]{:S(2)}, u32[]{:S(2)}) collective-permute-start(bf16[1040,128]{1,0:T(8,128)(2,1)S(1)} %newton.1.refs_0_), channel_id=1, source_target_pairs={{0,8},{2,10},{4,12},{6,14},{8,0},{10,2},{12,4},{14,6},{16,24},{18,... | collective-permute-start | bytes 798728 | tf_op jit(solution)/shard_map/ppermute | solution.py:40
  100.3 14.3 %collective-permute-start.16 = (bf16[1040,128]{1,0:T(8,128)(2,1)S(1)}, bf16[1040,128]{1,0:T(8,128)(2,1)S(1)}, u32[]{:S(2)}, u32[]{:S(2)}) collective-permute-start(bf16[1040,128]{1,0:T(8,128)(2,1)S(1)} %newton.1.refs_0_), channel_id=1, source_target_pairs={{0,24},{2,26},{4,28},{6,30},{8,16},{10,18},{12,20},{14,22},{16,8},... | collective-permute-start | bytes 798728 | tf_op jit(solution)/shard_map/ppermute | solution.py:40
  103.6 21.7 %collective-permute-start.15 = (bf16[1040,128]{1,0:T(8,128)(2,1)S(1)}, bf16[1040,128]{1,0:T(8,128)(2,1)S(1)}, u32[]{:S(2)}, u32[]{:S(2)}) collective-permute-start(bf16[1040,128]{1,0:T(8,128)(2,1)S(1)} %newton.1.refs_0_), channel_id=1, source_target_pairs={{0,16},{2,18},{4,20},{6,22},{8,24},{10,26},{12,28},{14,30},{16,0},... | collective-permute-start | bytes 798728 | tf_op jit(solution)/shard_map/ppermute | solution.py:40
  106.4 18.9 %collective-permute-start.21 = (bf16[1024,128]{1,0:T(8,128)(2,1)S(1)}, bf16[1024,128]{1,0:T(8,128)(2,1)S(1)}, u32[]{:S(2)}, u32[]{:S(2)}) collective-permute-start(bf16[1024,128]{1,0:T(8,128)(2,1)S(1)} %get-tuple-element.73), channel_id=1, source_target_pairs={{0,6},{2,0},{4,2},{6,4},{8,14},{10,8},{12,10},{14,12},{16,22},{18,... | collective-permute-start | bytes 786440 | tf_op jit(solution)/shard_map/ppermute | solution.py:35
  108.1 22.0 %collective-permute-start.25 = (bf16[1024,128]{1,0:T(8,128)(2,1)S(1)}, bf16[1024,128]{1,0:T(8,128)(2,1)S(1)}, u32[]{:S(2)}, u32[]{:S(2)}) collective-permute-start(bf16[1024,128]{1,0:T(8,128)(2,1)S(1)} %get-tuple-element.79), channel_id=1, source_target_pairs={{0,4},{2,6},{4,0},{6,2},{8,12},{10,14},{12,8},{14,10},{16,20},{18,... | collective-permute-start | bytes 786440 | tf_op jit(solution)/shard_map/ppermute | solution.py:35
  110.6 19.5 %collective-permute-start.26 = (bf16[1024,128]{1,0:T(8,128)(2,1)S(1)}, bf16[1024,128]{1,0:T(8,128)(2,1)S(1)}, u32[]{:S(2)}, u32[]{:S(2)}) collective-permute-start(bf16[1024,128]{1,0:T(8,128)(2,1)S(1)} %get-tuple-element.80), channel_id=1, source_target_pairs={{0,2},{2,4},{4,6},{6,0},{8,10},{10,12},{12,14},{14,8},{16,18},{18,... | collective-permute-start | bytes 786440 | tf_op jit(solution)/shard_map/ppermute | solution.py:35
  126.2 10.4 %collective-permute-start.22 = (bf16[1024,128]{1,0:T(8,128)(2,1)S(1)}, bf16[1024,128]{1,0:T(8,128)(2,1)S(1)}, u32[]{:S(2)}, u32[]{:S(2)}) collective-permute-start(bf16[1024,128]{1,0:T(8,128)(2,1)S(1)} %get-tuple-element.75), channel_id=1, source_target_pairs={{0,6},{2,0},{4,2},{6,4},{8,14},{10,8},{12,10},{14,12},{16,22},{18,... | collective-permute-start | bytes 786440 | tf_op jit(solution)/shard_map/ppermute | solution.py:35
  129.5 7.1 %collective-permute-start.23 = (bf16[1024,128]{1,0:T(8,128)(2,1)S(1)}, bf16[1024,128]{1,0:T(8,128)(2,1)S(1)}, u32[]{:S(2)}, u32[]{:S(2)}) collective-permute-start(bf16[1024,128]{1,0:T(8,128)(2,1)S(1)} %get-tuple-element.76), channel_id=1, source_target_pairs={{0,4},{2,6},{4,0},{6,2},{8,12},{10,14},{12,8},{14,10},{16,20},{18,... | collective-permute-start | bytes 786440 | tf_op jit(solution)/shard_map/ppermute | solution.py:35
  129.5 14.2 %collective-permute-start.24 = (bf16[1024,128]{1,0:T(8,128)(2,1)S(1)}, bf16[1024,128]{1,0:T(8,128)(2,1)S(1)}, u32[]{:S(2)}, u32[]{:S(2)}) collective-permute-start(bf16[1024,128]{1,0:T(8,128)(2,1)S(1)} %get-tuple-element.77), channel_id=1, source_target_pairs={{0,2},{2,4},{4,6},{6,0},{8,10},{10,12},{12,14},{14,8},{16,18},{18,... | collective-permute-start | bytes 786440 | tf_op jit(solution)/shard_map/ppermute | solution.py:35
